TPU v7x, 32 devices: a whole 2x2x4 slice. The times are simulated.
32 devices in a mesh: gx: 8 (over y, x, core), gy: 4 (over z).
Axes of the slice: x: 2, y: 2, z: 4, core: 2. Of those that a mesh axis runs over, the one named last changes fastest.
Arguments:
- right_side: float32 [128, 512], P('gx', 'gy'), may hold values from -18 to 18
- class_map: int32 [128, 512], P('gx', 'gy'), may hold values from 0 to 15
- class_values: float32 [16], replicated, may hold values from 0.3 to 30
- kept_counts: int32 [8, 4], P('gx', 'gy'), may hold values from 10 to 20
- factors: bfloat16 [8, 4, 18, 256, 256], P('gx', 'gy'), may hold values from -2 to 2
- basis: bfloat16 [8, 4, 20, 32, 144], P('gx', 'gy'), may hold values from -0.09375 to 0.09375
- coarse_factor: bfloat16 [640, 640], P(('gx', 'gy')), may hold values from -0.4375 to 0.4375
Outputs:
- solution_field: float32 [128, 512], P('gx', 'gy')
- residual: float32 [128, 512], P('gx', 'gy')
- preconditioned: float32 [128, 512], P('gx', 'gy')
Inputs may be any that keep to these rules, and one draw needn't show every extreme that they name: `kept_counts`: basis vectors of index 10 and above may be unused in a subdomain.
All inputs are finite; a program needn't handle non-finite values.
Results may differ from a plain program's by a relative error of at most 0.023.
Values may be sent and summed in bfloat16 or wider, within the bound.
A program may use at most 64 MiB of HBM per device.

v0:
```python
import jax
import jax.numpy as jnp
from jax import lax
from jax.sharding import PartitionSpec as P

OV = 8
ITERS = 3


def extended_2(shard, sides, width):
    for axis, dim in sides:
        devices, length = (lax.axis_size(axis), shard.shape[dim])
        up = [(i, (i + 1) % devices) for i in range(devices - 1)]
        down = [(j, i) for i, j in up]
        last = lax.slice_in_dim(shard, length - width, length, axis=dim)
        initial = lax.slice_in_dim(shard, 0, width, axis=dim)
        before = lax.ppermute(last, axis, up)
        after = lax.ppermute(initial, axis, down)
        shard = jnp.concatenate([before, shard, after], axis=dim)
    return shard


def fold_axis(padded, size, axis):
    own = lax.slice_in_dim(padded, 2 * OV, 2 * OV + size, axis=axis)
    lower = lax.slice_in_dim(padded, 0, OV, axis=axis)
    upper = lax.slice_in_dim(padded, size + 3 * OV, size + 4 * OV, axis=axis)
    widths_low = [(0, 0), (0, 0)]
    widths_high = [(0, 0), (0, 0)]
    widths_low[axis] = (0, size - OV)
    widths_high[axis] = (size - OV, 0)
    return own + jnp.pad(lower, widths_low) + jnp.pad(upper, widths_high)


def per_device(right_side, class_map, class_values, kept_counts, factors, basis, coarse_factor):
    rows, columns = right_side.shape
    levels = jnp.arange(class_values.shape[0], dtype=jnp.int32)
    chosen = class_map[None, :, :] == levels[:, None, None]
    conductivity = jnp.sum(jnp.where(chosen, class_values[:, None, None], 0.0), axis=0)
    conductivity_rim = extended_2(conductivity, (("gx", 0), ("gy", 1)), 1)
    face_north = 0.5 * (conductivity + conductivity_rim[:-2, 1:-1])
    face_south = 0.5 * (conductivity + conductivity_rim[2:, 1:-1])
    face_west = 0.5 * (conductivity + conductivity_rim[1:-1, :-2])
    face_east = 0.5 * (conductivity + conductivity_rim[1:-1, 2:])
    blocks = factors[0, 0]
    vectors = basis[0, 0]
    modes = vectors.shape[0]
    keep = (jnp.arange(modes, dtype=jnp.int32) < kept_counts[0, 0]).astype(jnp.float32)

    def coarse_solve(coarse_in):
        across = lax.all_gather(coarse_in.reshape(1, modes), "gy", axis=0, tiled=True)
        gathered = lax.all_gather(across.reshape(1, -1), "gx", axis=0, tiled=True)
        coarse_mid = (
            jnp.dot(coarse_factor, gathered.reshape(-1), preferred_element_type=jnp.float32) * keep
        )
        mid_half = coarse_mid.astype(jnp.bfloat16)
        term = jnp.dot(mid_half, coarse_factor, preferred_element_type=jnp.float32)
        term = term.reshape(lax.axis_size("gx"), lax.axis_size("gy"), modes)
        partial_rows = lax.psum_scatter(
            term.astype(jnp.bfloat16), "gy", scatter_dimension=1, tiled=True
        ).astype(jnp.float32)
        coarse_out = (
            lax.psum_scatter(partial_rows, "gx", scatter_dimension=0, tiled=True).reshape(modes)
            * keep
        )
        return (coarse_mid, mid_half, coarse_out)

    def combine(total):
        folded = extended_2(total, (("gx", 0), ("gy", 1)), OV)
        return fold_axis(fold_axis(folded, rows, 0), columns, 1)

    def precondition(residual):
        rounded = residual.astype(jnp.bfloat16)
        extended = extended_2(rounded, (("gx", 0), ("gy", 1)), OV)
        ext_rows, ext_columns = extended.shape
        flat = extended.reshape(blocks.shape[0], blocks.shape[1])
        solved = jnp.einsum("bij,bj->bi", blocks, flat, preferred_element_type=jnp.float32)
        solved_half = solved.astype(jnp.bfloat16)
        local_part = jnp.einsum(
            "bij,bi->bj", blocks, solved_half, preferred_element_type=jnp.float32
        )
        local_part = local_part.reshape(ext_rows, ext_columns)
        restricted = (
            jnp.einsum("kxy,xy->k", vectors, extended, preferred_element_type=jnp.float32) * keep
        )
        coarse_mid, mid_half, coarse_out = coarse_solve(restricted.astype(jnp.bfloat16))
        weights = coarse_out.astype(jnp.bfloat16)
        total = local_part + jnp.einsum(
            "k,kxy->xy", weights, vectors, preferred_element_type=jnp.float32
        )
        result = combine(total)
        energy = lax.psum(jnp.sum(residual * result), ("gx", "gy"))
        return (result, energy)

    solution_field = jnp.zeros_like(right_side)
    residual = right_side
    preconditioned, energy = precondition(residual)
    direction = preconditioned
    for step in range(ITERS):
        padded = extended_2(direction, (("gx", 0), ("gy", 1)), 1)
        image = (
            face_north * (direction - padded[:-2, 1:-1])
            + face_south * (direction - padded[2:, 1:-1])
            + face_west * (direction - padded[1:-1, :-2])
            + face_east * (direction - padded[1:-1, 2:])
        )
        curvature = lax.psum(jnp.sum(direction * image), ("gx", "gy"))
        step_length = energy / curvature
        solution_field = solution_field + step_length * direction
        residual = residual - step_length * image
        preconditioned, fresh = precondition(residual)
        if step + 1 < ITERS:
            direction = preconditioned + fresh / energy * direction
            energy = fresh
    return (solution_field, residual, preconditioned)


def solution(mesh):
    in_specs = (
        P("gx", "gy"),
        P("gx", "gy"),
        P(),
        P("gx", "gy"),
        P("gx", "gy", None, None, None),
        P("gx", "gy", None, None, None),
        P(("gx", "gy"), None),
    )
    out_specs = (P("gx", "gy"), P("gx", "gy"), P("gx", "gy"))
    return jax.shard_map(
        per_device, mesh=mesh, in_specs=in_specs, out_specs=out_specs, check_vma=False
    )
```

profile of v0, /device:TPU:0, one launch (start us, length us, event | category | flops | bytes accessed | tf_op | source)
XLA Modules:
  0.0 628.8 jit_solution(17202752126834333796)
XLA Ops:
  8.0 5.6 collective-permute-start.2
  19.1 11.1 %all-reduce.8 = bf16[80]{0:T(256)(128)(2,1)S(1)} all-reduce(bf16[80]{0:T(256)(128)(2,1)S(1)} %dynamic-update-slice), channel_id=2, replica_groups=mesh['gx'=8,'gy'=4] {'gy'}, use_global_device_ids=true, to_apply=%add.8 | all-reduce | flops 80 | bytes 320
  30.4 12.9 %all-reduce.9 = bf16[640]{0:T(1024)(128)(2,1)S(1)} all-reduce(bf16[640]{0:T(1024)(128)(2,1)S(1)} %dynamic-update-slice.1), channel_id=6, replica_groups=mesh['gx'=8,'gy'=4] {'gx'}, use_global_device_ids=true, to_apply=%add.9 | all-reduce | flops 640 | bytes 2560
  43.6 8.5 %all-reduce.16 = bf16[8,4,20]{2,0,1:T(8,128)(2,1)S(1)} all-reduce(bf16[8,4,20]{2,0,1:T(8,128)(2,1)S(1)} %copy.22), channel_id=10, replica_groups=mesh['gx'=8,'gy'=4] {'gy'}, use_global_device_ids=true, to_apply=%region_0.1.clone | all-reduce | flops 640 | bytes 2560
  52.9 22.4 %all-reduce.17 = bf16[8,1,20]{2,1,0:T(2,128)(2,1)S(1)} all-reduce(f32[8,1,20]{2,1,0:T(1,128)S(1)} %bitcast.232), channel_id=11, replica_groups=mesh['gx'=8,'gy'=4] {'gx'}, use_global_device_ids=true, to_apply=%region_1.2.clone | all-reduce | flops 160 | bytes 960
  86.8 4.5 collective-permute-start.6
  105.2 4.5 collective-permute-start.13
  111.9 45.1 %all-reduce.24 = (f32[]{:T(128)}, f32[]{:T(128)}) all-reduce(f32[]{:T(128)} %get-tuple-element.4, f32[]{:T(128)} %get-tuple-element.3), channel_id=1, replica_groups=mesh['gx'=8,'gy'=4] {'gx','gy'}, use_global_device_ids=true, to_apply=%region_3.4 | all-reduce | flops 2 | bytes 16 | tf_op jit(solution)/shard_map/psum | solution.py:91
  172.8 12.4 %all-reduce.10 = bf16[80]{0:T(256)(128)(2,1)S(1)} all-reduce(bf16[80]{0:T(256)(128)(2,1)S(1)} %dynamic-update-slice.2), channel_id=3, replica_groups=mesh['gx'=8,'gy'=4] {'gy'}, use_global_device_ids=true, to_apply=%add.10 | all-reduce | flops 80 | bytes 320
  185.4 14.4 %all-reduce.11 = bf16[640]{0:T(1024)(128)(2,1)S(1)} all-reduce(bf16[640]{0:T(1024)(128)(2,1)S(1)} %dynamic-update-slice.3), channel_id=7, replica_groups=mesh['gx'=8,'gy'=4] {'gx'}, use_global_device_ids=true, to_apply=%add.11 | all-reduce | flops 640 | bytes 2560
  200.2 8.5 %all-reduce.18 = bf16[8,4,20]{2,0,1:T(8,128)(2,1)S(1)} all-reduce(bf16[8,4,20]{2,0,1:T(8,128)(2,1)S(1)} %copy.24), channel_id=12, replica_groups=mesh['gx'=8,'gy'=4] {'gy'}, use_global_device_ids=true, to_apply=%region_7.8.clone | all-reduce | flops 640 | bytes 2560
  209.4 22.4 %all-reduce.19 = bf16[8,1,20]{2,1,0:T(2,128)(2,1)S(1)} all-reduce(f32[8,1,20]{2,1,0:T(1,128)S(1)} %bitcast.233), channel_id=13, replica_groups=mesh['gx'=8,'gy'=4] {'gx'}, use_global_device_ids=true, to_apply=%region_8.9.clone | all-reduce | flops 160 | bytes 960
  246.3 44.6 %psum.44 = f32[]{:T(128)} all-reduce(f32[]{:T(128)} %multiply_reduce_fusion.3), channel_id=1, replica_groups=mesh['gx'=8,'gy'=4] {'gx','gy'}, use_global_device_ids=true, to_apply=%region_10.11 | all-reduce | flops 1 | bytes 8 | tf_op jit(solution)/shard_map/psum | solution.py:91
  305.5 44.3 %psum.45 = f32[]{:T(128)} all-reduce(f32[]{:T(128)} %get-tuple-element.13), channel_id=1, replica_groups=mesh['gx'=8,'gy'=4] {'gx','gy'}, use_global_device_ids=true, to_apply=%region_12.13 | all-reduce | flops 1 | bytes 8 | tf_op jit(solution)/shard_map/psum | solution.py:106
  365.5 10.9 %all-reduce.12 = bf16[80]{0:T(256)(128)(2,1)S(1)} all-reduce(bf16[80]{0:T(256)(128)(2,1)S(1)} %dynamic-update-slice.4), channel_id=4, replica_groups=mesh['gx'=8,'gy'=4] {'gy'}, use_global_device_ids=true, to_apply=%add.12 | all-reduce | flops 80 | bytes 320
  376.7 13.9 %all-reduce.13 = bf16[640]{0:T(1024)(128)(2,1)S(1)} all-reduce(bf16[640]{0:T(1024)(128)(2,1)S(1)} %dynamic-update-slice.5), channel_id=8, replica_groups=mesh['gx'=8,'gy'=4] {'gx'}, use_global_device_ids=true, to_apply=%add.13 | all-reduce | flops 640 | bytes 2560
  391.0 8.5 %all-reduce.20 = bf16[8,4,20]{2,0,1:T(8,128)(2,1)S(1)} all-reduce(bf16[8,4,20]{2,0,1:T(8,128)(2,1)S(1)} %copy.26), channel_id=14, replica_groups=mesh['gx'=8,'gy'=4] {'gy'}, use_global_device_ids=true, to_apply=%region_13.14.clone | all-reduce | flops 640 | bytes 2560
  400.2 22.5 %all-reduce.21 = bf16[8,1,20]{2,1,0:T(2,128)(2,1)S(1)} all-reduce(f32[8,1,20]{2,1,0:T(1,128)S(1)} %bitcast.234), channel_id=15, replica_groups=mesh['gx'=8,'gy'=4] {'gx'}, use_global_device_ids=true, to_apply=%region_14.15.clone | all-reduce | flops 160 | bytes 960
  437.4 44.6 %psum.46 = f32[]{:T(128)} all-reduce(f32[]{:T(128)} %multiply_reduce_fusion.1), channel_id=1, replica_groups=mesh['gx'=8,'gy'=4] {'gx','gy'}, use_global_device_ids=true, to_apply=%region_16.17 | all-reduce | flops 1 | bytes 8 | tf_op jit(solution)/shard_map/psum | solution.py:91
  496.5 44.3 %psum.47 = f32[]{:T(128)} all-reduce(f32[]{:T(128)} %get-tuple-element.9), channel_id=1, replica_groups=mesh['gx'=8,'gy'=4] {'gx','gy'}, use_global_device_ids=true, to_apply=%region_18.19 | all-reduce | flops 1 | bytes 8 | tf_op jit(solution)/shard_map/psum | solution.py:106
  557.2 10.9 %all-reduce.14 = bf16[80]{0:T(256)(128)(2,1)S(1)} all-reduce(bf16[80]{0:T(256)(128)(2,1)S(1)} %dynamic-update-slice.6), channel_id=5, replica_groups=mesh['gx'=8,'gy'=4] {'gy'}, use_global_device_ids=true, to_apply=%add.14 | all-reduce | flops 80 | bytes 320
  568.4 13.9 %all-reduce.15 = bf16[640]{0:T(1024)(128)(2,1)S(1)} all-reduce(bf16[640]{0:T(1024)(128)(2,1)S(1)} %dynamic-update-slice.7), channel_id=9, replica_groups=mesh['gx'=8,'gy'=4] {'gx'}, use_global_device_ids=true, to_apply=%add.15 | all-reduce | flops 640 | bytes 2560
  582.7 8.5 %all-reduce.22 = bf16[8,4,20]{2,0,1:T(8,128)(2,1)S(1)} all-reduce(bf16[8,4,20]{2,0,1:T(8,128)(2,1)S(1)} %copy.28), channel_id=16, replica_groups=mesh['gx'=8,'gy'=4] {'gy'}, use_global_device_ids=true, to_apply=%region_19.20.clone | all-reduce | flops 640 | bytes 2560
  591.9 22.4 %all-reduce.23 = bf16[8,1,20]{2,1,0:T(2,128)(2,1)S(1)} all-reduce(f32[8,1,20]{2,1,0:T(1,128)S(1)} %bitcast.231), channel_id=17, replica_groups=mesh['gx'=8,'gy'=4] {'gx'}, use_global_device_ids=true, to_apply=%region_20.21.clone | all-reduce | flops 160 | bytes 960
  (249 shorter events, 157.0 us)
Async XLA Ops:
  6.7 10.2 %collective-permute-start.3 = (bf16[32,8]{1,0:T(8,128)(2,1)S(1)}, bf16[32,8]{1,0:T(8,128)(2,1)S(1)}, u32[]{:S(2)}, u32[]{:S(2)}) collective-permute-start(bf16[32,8]{1,0:T(8,128)(2,1)S(1)} %get-tuple-element.57), channel_id=1, source_target_pairs={{1,0},{2,1},{3,2},{5,4},{6,5},{7,6},{9,8},{10,9},{11,10},{13,12},{... | collective-permute-start | bytes 1544 | tf_op jit(solution)/shard_map/ppermute | solution.py:18
  8.0 8.9 %collective-permute-start.2 = (bf16[32,8]{1,0:T(8,128)(2,1)S(1)}, bf16[32,8]{1,0:T(8,128)(2,1)S(1)}, u32[]{:S(2)}, u32[]{:S(2)}) collective-permute-start(bf16[32,8]{1,0:T(8,128)(2,1)S(1)} %get-tuple-element.56), channel_id=1, source_target_pairs={{0,1},{1,2},{2,3},{4,5},{5,6},{6,7},{8,9},{9,10},{10,11},{12,13},{... | collective-permute-start | bytes 1544 | tf_op jit(solution)/shard_map/ppermute | solution.py:17
  76.3 9.0 %collective-permute-start.5 = (f32[8,144]{1,0:T(8,128)S(1)}, f32[8,144]{1,0:T(8,128)S(1)}, u32[]{:S(2)}, u32[]{:S(2)}) collective-permute-start(f32[8,144]{1,0:T(8,128)S(1)} %get-tuple-element.33), channel_id=1, source_target_pairs={{4,0},{8,4},{12,8},{16,12},{20,16},{24,20},{28,24},{5,1},{9,5},{13... | collective-permute-start | bytes 13832 | tf_op jit(solution)/shard_map/ppermute | solution.py:18
  77.6 7.7 %collective-permute-start.4 = (f32[8,144]{1,0:T(8,128)S(1)}, f32[8,144]{1,0:T(8,128)S(1)}, u32[]{:S(2)}, u32[]{:S(2)}) collective-permute-start(f32[8,144]{1,0:T(8,128)S(1)} %get-tuple-element.32), channel_id=1, source_target_pairs={{0,4},{4,8},{8,12},{12,16},{16,20},{20,24},{24,28},{1,5},{5,9},{9,... | collective-permute-start | bytes 13832 | tf_op jit(solution)/shard_map/ppermute | solution.py:17
  80.7 10.6 %collective-permute-start.10 = (f32[1,128]{1,0:T(1,128)S(1)}, f32[1,128]{1,0:T(1,128)S(1)}, u32[]{:S(2)}, u32[]{:S(2)}) collective-permute-start(f32[1,128]{1,0:T(1,128)S(1)} %get-tuple-element.53), channel_id=1, source_target_pairs={{4,0},{8,4},{12,8},{16,12},{20,16},{24,20},{28,24},{5,1},{9,5},{13... | collective-permute-start | bytes 1544 | tf_op jit(solution)/shard_map/ppermute | solution.py:18
  82.0 9.4 %collective-permute-start.8 = (f32[1,128]{1,0:T(1,128)S(1)}, f32[1,128]{1,0:T(1,128)S(1)}, u32[]{:S(2)}, u32[]{:S(2)}) collective-permute-start(f32[1,128]{1,0:T(1,128)S(1)} %get-tuple-element.52), channel_id=1, source_target_pairs={{0,4},{4,8},{8,12},{12,16},{16,20},{20,24},{24,28},{1,5},{5,9},{9,... | collective-permute-start | bytes 1544 | tf_op jit(solution)/shard_map/ppermute | solution.py:17
  85.5 5.9 collective-permute-start.7
  86.8 6.1 collective-permute-start.6
  93.2 10.6 %collective-permute-start.11 = (f32[1,128]{1,0:T(1,128)S(1)}, f32[1,128]{1,0:T(1,128)S(1)}, u32[]{:S(2)}, u32[]{:S(2)}) collective-permute-start(f32[1,128]{1,0:T(1,128)S(1)} %get-tuple-element.55), channel_id=1, source_target_pairs={{4,0},{8,4},{12,8},{16,12},{20,16},{24,20},{28,24},{5,1},{9,5},{13... | collective-permute-start | bytes 1544 | tf_op jit(solution)/shard_map/ppermute | solution.py:18
  94.5 9.3 %collective-permute-start.9 = (f32[1,128]{1,0:T(1,128)S(1)}, f32[1,128]{1,0:T(1,128)S(1)}, u32[]{:S(2)}, u32[]{:S(2)}) collective-permute-start(f32[1,128]{1,0:T(1,128)S(1)} %get-tuple-element.54), channel_id=1, source_target_pairs={{0,4},{4,8},{8,12},{12,16},{16,20},{20,24},{24,28},{1,5},{5,9},{9,... | collective-permute-start | bytes 1544 | tf_op jit(solution)/shard_map/ppermute | solution.py:17
  97.9 11.8 %collective-permute-start.14 = (f32[18,1]{1,0:T(8,128)S(1)}, f32[18,1]{1,0:T(8,128)S(1)}, u32[]{:S(2)}, u32[]{:S(2)}) collective-permute-start(f32[18,1]{1,0:T(8,128)S(1)} %get-tuple-element.39), channel_id=1, source_target_pairs={{1,0},{2,1},{3,2},{5,4},{6,5},{7,6},{9,8},{10,9},{11,10},{13,12},{... | collective-permute-start | bytes 224 | tf_op jit(solution)/shard_map/ppermute | solution.py:18
  99.2 10.5 %collective-permute-start.12 = (f32[18,1]{1,0:T(8,128)S(1)}, f32[18,1]{1,0:T(8,128)S(1)}, u32[]{:S(2)}, u32[]{:S(2)}) collective-permute-start(f32[18,1]{1,0:T(8,128)S(1)} %get-tuple-element.38), channel_id=1, source_target_pairs={{0,1},{1,2},{2,3},{4,5},{5,6},{6,7},{8,9},{9,10},{10,11},{12,13},{... | collective-permute-start | bytes 224 | tf_op jit(solution)/shard_map/ppermute | solution.py:17
  103.9 5.9 collective-permute-start.15
  105.2 5.9 collective-permute-start.13
  164.8 5.9 collective-permute-start.18
  239.3 6.1 collective-permute-start.22
  298.8 5.9 collective-permute-start.26
  357.6 5.9 collective-permute-start.30
  429.0 5.8 collective-permute-start.35
  430.3 6.1 collective-permute-start.34
  489.9 5.9 collective-permute-start.38
  549.3 5.9 collective-permute-start.42
  620.5 6.5 %collective-permute-start.47 = (f32[48,8]{1,0:T(8,128)S(1)}, f32[48,8]{1,0:T(8,128)S(1)}, u32[]{:S(2)}, u32[]{:S(2)}) collective-permute-start(f32[48,8]{1,0:T(8,128)S(1)} %get-tuple-element.19), channel_id=1, source_target_pairs={{1,0},{2,1},{3,2},{5,4},{6,5},{7,6},{9,8},{10,9},{11,10},{13,12},{... | collective-permute-start | bytes 4616 | tf_op jit(solution)/shard_map/ppermute | solution.py:18
  621.8 6.1 collective-permute-start.46
  (30 other events, 396.9 us)
where the time goes:
time: 635 us; the launch traced here: 629 us
  blocking collectives  447 us (70%)
  starting transfers between devices  123 us (19%)
  waiting for transfers between devices  19.9 us (3%)
  other arithmetic  11.6 us (2%)
  matrix products  10.9 us (2%)
  between operations  10.1 us (2%)
    unnamed x16, blocking collectives  224 us
    psum x3, blocking collectives, precondition(): energy = lax.psum(jnp.sum(residual * result), ('gx', 'gy'))  134 us
    ppermute x24, starting transfers between devices, extended_2(): before = lax.ppermute(last, axis, up)  92.6 us
    psum x2, blocking collectives, per_device(): curvature = lax.psum(jnp.sum(direction * image), ('gx', 'gy'))  88.6 us
    ppermute x24, starting transfers between devices, extended_2(): after = lax.ppermute(initial, axis, down)  30.8 us
    ppermute x24, waiting for transfers between devices, extended_2(): before = lax.ppermute(last, axis, up)  19.8 us
  transfers between devices with their start and end apart: 48, of which 18 were waited for; matrix products, arithmetic and copies ran while one was open for 0% of the time, Pallas kernels for 0%

commit v1 on v0

v1 whole, which is shorter than its diff:
```python
import functools

import jax
import jax.numpy as jnp
from jax import lax
from jax.experimental import pallas as pl
from jax.experimental.pallas import tpu as pltpu
from jax.sharding import PartitionSpec as P

OV = 8
ITERS = 3
LANES = 128
MODES = 32
MESH = pl.DeviceIdType.MESH
SIDES = tuple((a, b) for a in (-1, 0, 1) for b in (-1, 0, 1) if (a, b) != (0, 0))
NT = (((1,), (1,)), ((), ()))
NN = (((1,), (0,)), ((), ()))


def kernel(
    shape,
    right_ref,
    class_ref,
    values_ref,
    kept_ref,
    factors_ref,
    basis_ref,
    coarse_ref,
    field_out,
    residual_out,
    pre_out,
    cond,
    frames,
    fold,
    total,
    natural,
    flat,
    solved,
    message,
    terms,
    gathered,
    scattered,
    halo_send,
    halo_recv,
    fold_send,
    fold_recv,
    gather_send,
    gather_recv,
    scatter_send,
    scatter_recv,
):
    nx, ny = shape
    count = nx * ny
    rows, columns = right_ref.shape
    blocks, block = factors_ref.shape[:2]
    ext_rows, ext_columns = rows + 2 * OV, columns + 2 * OV
    ax, ay = lax.axis_index("gx"), lax.axis_index("gy")
    me = ax * ny + ay
    own = (pl.ds(rows, rows), pl.ds(columns, columns))

    def place(number):
        return (number // ny, number % ny)

    def present(da, db):
        checks = []
        if da:
            checks.append(ax > 0 if da < 0 else ax < nx - 1)
        if db:
            checks.append(ay > 0 if db < 0 else ay < ny - 1)
        return checks[0] if len(checks) == 1 else jnp.logical_and(*checks)

    def patch(ref, da, db):
        return ref.at[pl.ds((1 + da) * rows, rows), pl.ds((1 + db) * columns, columns)]

    def halo_copy(ref, slot, index):
        da, db = SIDES[index]
        return pltpu.make_async_remote_copy(
            src_ref=patch(ref, 0, 0),
            dst_ref=patch(ref, -da, -db),
            send_sem=halo_send.at[slot, index],
            recv_sem=halo_recv.at[slot, index],
            device_id=(ax + da, ay + db),
            device_id_type=MESH,
        )

    def fold_copy(slot, index):
        da, db = SIDES[index]
        return pltpu.make_async_remote_copy(
            src_ref=patch(total, da, db),
            dst_ref=fold.at[slot, index],
            send_sem=fold_send.at[slot, index],
            recv_sem=fold_recv.at[slot, index],
            device_id=(ax + da, ay + db),
            device_id_type=MESH,
        )

    def start_sides(make):
        for index, (da, db) in enumerate(SIDES):

            @pl.when(present(da, db))
            def _(index=index):
                make(index).start()

    def wait_sides(make):
        for index, (da, db) in enumerate(SIDES):

            @pl.when(present(-da, -db))
            def _(index=index):
                make(index).wait_recv()

    def drain_sides(make):
        for index, (da, db) in enumerate(SIDES):

            @pl.when(present(da, db))
            def _(index=index):
                make(index).wait_send()

    def gather_copy(slot, source, target):
        return pltpu.make_async_remote_copy(
            src_ref=message.at[slot],
            dst_ref=gathered.at[slot, source],
            send_sem=gather_send.at[slot],
            recv_sem=gather_recv.at[slot],
            device_id=place(target),
            device_id_type=MESH,
        )

    def scatter_copy(slot, source, target):
        return pltpu.make_async_remote_copy(
            src_ref=terms.at[slot, target],
            dst_ref=scattered.at[slot, source],
            send_sem=scatter_send.at[slot],
            recv_sem=scatter_recv.at[slot],
            device_id=place(target),
            device_id_type=MESH,
        )

    def everything(ref, send, recv, slot):
        span = ref.at[slot, pl.ds(0, count - 1)]
        return pltpu.make_async_remote_copy(
            src_ref=span,
            dst_ref=span,
            send_sem=send.at[slot],
            recv_sem=recv.at[slot],
            device_id=place(lax.rem(me + 1, count)),
            device_id_type=MESH,
        )

    def others(act):
        def one(offset, carry):
            act(lax.rem(me + offset, count))
            return carry

        lax.fori_loop(1, count, one, 0)

    frames[...] = jnp.zeros_like(frames)
    cond[...] = jnp.zeros_like(cond)
    fold[...] = jnp.zeros_like(fold)
    total[...] = jnp.zeros_like(total)
    natural[...] = jnp.zeros_like(natural)
    right = right_ref[...]
    classes = class_ref[...]
    conductivity = jnp.zeros((rows, columns), jnp.float32)
    for level in range(values_ref.shape[0]):
        conductivity = jnp.where(classes == level, values_ref[level], conductivity)
    cond[own] = conductivity
    frames[(0,) + own] = right

    barrier = pltpu.get_barrier_semaphore()
    others(
        lambda target: pl.semaphore_signal(
            barrier, inc=1, device_id=place(target), device_id_type=MESH
        )
    )
    pl.semaphore_wait(barrier, count - 1)

    start_sides(lambda index: halo_copy(frames.at[0], 0, index))
    start_sides(lambda index: halo_copy(cond, ITERS + 1, index))

    frame_shape = cond.shape
    row_at = lax.broadcasted_iota(jnp.int32, frame_shape, 0) + (ax - 1) * rows
    column_at = lax.broadcasted_iota(jnp.int32, frame_shape, 1) + (ay - 1) * columns
    inside = (row_at >= 0) & (row_at < nx * rows) & (column_at >= 0) & (column_at < ny * columns)
    lane = lax.broadcasted_iota(jnp.int32, (1, LANES), 1)
    keep = jnp.where(lane < kept_ref[...], 1.0, 0.0)
    keep_modes = keep[:, :MODES]

    def lane_value(row, index):
        return jnp.sum(jnp.where(lane == index, row, 0.0), axis=1, keepdims=True)

    def whole_sum(values):
        return jnp.sum(jnp.sum(values, axis=0, keepdims=True), axis=1, keepdims=True)

    def precondition(slot, values, scalars):
        wide = frame_shape[1]
        rolled = pltpu.roll(values, wide - (columns - OV), 1)
        natural[...] = rolled[rows - OV : rows - OV + ext_rows]
        for row in range(ext_rows):
            flat[0:1, ext_columns * row : ext_columns * (row + 1)] = natural[
                row : row + 1, 0:ext_columns
            ]
        box = flat[...].astype(jnp.bfloat16)
        coarse_in = lax.dot_general(
            box, basis_ref[...], NT, preferred_element_type=jnp.float32
        )
        row = jnp.zeros((1, LANES), jnp.float32)
        for index, scalar in enumerate(scalars):
            row = jnp.where(lane == MODES + index, scalar, row)
        message[slot] = row
        message[slot, :, 0:MODES] = coarse_in * keep_modes
        others(lambda target: gather_copy(slot, me, target).start())
        gathered[slot, me] = message[slot]
        for index in range(blocks):
            at = slice(index * block, (index + 1) * block)
            half = lax.dot_general(
                box[:, at], factors_ref[index], NT, preferred_element_type=jnp.float32
            ).astype(jnp.bfloat16)
            solved[0:1, at] = lax.dot_general(
                half, factors_ref[index], NN, preferred_element_type=jnp.float32
            )
        everything(gathered, gather_send, gather_recv, slot).wait_recv()
        sums = jnp.sum(gathered[slot], axis=0)
        everyone = jnp.concatenate(
            [gathered[slot, index] for index in range(count)], axis=1
        ).astype(jnp.bfloat16)
        coarse_mid = lax.dot_general(
            everyone, coarse_ref[...], NT, preferred_element_type=jnp.float32
        )
        mid_half = (coarse_mid * keep_modes).astype(jnp.bfloat16)
        spread = lax.dot_general(
            mid_half, coarse_ref[...], NN, preferred_element_type=jnp.float32
        )
        for index in range(count):
            terms[slot, index] = spread[:, index * LANES : (index + 1) * LANES]
        others(lambda target: scatter_copy(slot, me, target).start())
        scattered[slot, me] = terms[slot, me]
        everything(scattered, scatter_send, scatter_recv, slot).wait_recv()
        coarse_out = jnp.sum(scattered[slot], axis=0) * keep
        weights = coarse_out[:, :MODES].astype(jnp.bfloat16)
        solved[...] += lax.dot_general(
            weights, basis_ref[...], NN, preferred_element_type=jnp.float32
        )
        for row in range(ext_rows):
            natural[row : row + 1, 0:ext_columns] = solved[
                0:1, ext_columns * row : ext_columns * (row + 1)
            ]
        lanes = lax.broadcasted_iota(jnp.int32, natural.shape, 1)
        clean = jnp.where(lanes < ext_columns, natural[...], 0.0)
        total[rows - OV : rows - OV + ext_rows, :] = pltpu.roll(clean, columns - OV, 1)
        copies = functools.partial(fold_copy, slot)
        start_sides(copies)
        result = total[own]
        wait_sides(copies)
        for index in range(len(SIDES)):
            result = result + fold[slot, index]
        drain_sides(copies)
        return result, sums

    copies = lambda index: halo_copy(frames.at[0], 0, index)
    wait_sides(copies)
    drain_sides(copies)
    zero = jnp.zeros((1, 1), jnp.float32)
    z, _ = precondition(0, frames[0], (zero,))

    copies = lambda index: halo_copy(cond, ITERS + 1, index)
    wait_sides(copies)
    drain_sides(copies)
    cells = cond[...]
    face_north = 0.5 * (cells + pltpu.roll(cells, 1, 0))
    face_west = 0.5 * (cells + pltpu.roll(cells, 1, 1))

    def operate(field):
        north = face_north * (field - pltpu.roll(field, 1, 0))
        west = face_west * (field - pltpu.roll(field, 1, 1))
        image = north - pltpu.roll(north, frame_shape[0] - 1, 0)
        image = image + (west - pltpu.roll(west, frame_shape[1] - 1, 1))
        return jnp.where(inside, image, 0.0)

    residual = right
    field = jnp.zeros_like(right)
    direction = image = mapped = None
    energy = curvature = None
    for step in range(1, ITERS + 1):
        frames[(step,) + own] = z
        copies = functools.partial(halo_copy, frames.at[step], step)
        start_sides(copies)
        wait_sides(copies)
        drain_sides(copies)
        applied = operate(frames[step])
        applied_own = applied[rows : 2 * rows, columns : 2 * columns]
        scalars = [whole_sum(residual * z), whole_sum(z * applied_own)]
        if step > 1:
            scalars.append(whole_sum(z * image))
        corrected, sums = precondition(step, applied, scalars)
        fresh, plain = lane_value(sums, MODES), lane_value(sums, MODES + 1)
        if step == 1:
            direction, image, mapped, curvature = z, applied_own, corrected, plain
        else:
            ratio = fresh / energy
            cross = lane_value(sums, MODES + 2)
            curvature = plain + 2.0 * ratio * cross + ratio * ratio * curvature
            direction = z + ratio * direction
            image = applied_own + ratio * image
            mapped = corrected + ratio * mapped
        energy = fresh
        length = energy / curvature
        field = field + length * direction
        residual = residual - length * image
        z = z - length * mapped

    field_out[...] = field
    residual_out[...] = residual
    pre_out[...] = z

    for slot in range(ITERS + 1):
        everything(gathered, gather_send, gather_recv, slot).wait_send()
        everything(terms, scatter_send, scatter_recv, slot).wait_send()


def per_device(
    shape, right_side, class_map, class_values, kept_counts, factors, basis, coarse_factor
):
    count = shape[0] * shape[1]
    rows, columns = right_side.shape
    modes = basis.shape[2]
    blocks, block = factors.shape[2:4]
    cells = blocks * block
    flat_basis = jnp.pad(basis.reshape(modes, cells), ((0, MODES - modes), (0, 0)))
    spaced = coarse_factor.reshape(modes, count, modes)
    spaced = jnp.pad(spaced, ((0, MODES - modes), (0, 0), (0, LANES - modes)))
    spaced = spaced.reshape(MODES, count * LANES)
    steps = ITERS + 1
    frame = (3 * rows, 3 * columns)
    vmem = pl.BlockSpec(memory_space=pltpu.VMEM)
    smem = pl.BlockSpec(memory_space=pltpu.SMEM)
    f32 = jnp.float32
    return pl.pallas_call(
        functools.partial(kernel, shape),
        out_shape=(jax.ShapeDtypeStruct((rows, columns), f32),) * 3,
        in_specs=[vmem, vmem, smem, vmem, vmem, vmem, vmem],
        out_specs=(vmem,) * 3,
        scratch_shapes=[
            pltpu.VMEM(frame, f32),
            pltpu.VMEM((steps,) + frame, f32),
            pltpu.VMEM((steps, len(SIDES), rows, columns), f32),
            pltpu.VMEM(frame, f32),
            pltpu.VMEM((rows + 2 * OV, 3 * columns), f32),
            pltpu.VMEM((1, cells), f32),
            pltpu.VMEM((1, cells), f32),
            pltpu.VMEM((steps, 1, LANES), f32),
            pltpu.VMEM((steps, count, 1, LANES), f32),
            pltpu.VMEM((steps, count, 1, LANES), f32),
            pltpu.VMEM((steps, count, 1, LANES), f32),
            pltpu.SemaphoreType.DMA((steps + 1, len(SIDES))),
            pltpu.SemaphoreType.DMA((steps + 1, len(SIDES))),
            pltpu.SemaphoreType.DMA((steps, len(SIDES))),
            pltpu.SemaphoreType.DMA((steps, len(SIDES))),
            pltpu.SemaphoreType.DMA((steps,)),
            pltpu.SemaphoreType.DMA((steps,)),
            pltpu.SemaphoreType.DMA((steps,)),
            pltpu.SemaphoreType.DMA((steps,)),
        ],
        compiler_params=pltpu.CompilerParams(
            collective_id=0, has_side_effects=True, vmem_limit_bytes=40 * 2**20
        ),
    )(
        right_side,
        class_map,
        class_values,
        kept_counts,
        factors.reshape(blocks, block, block),
        flat_basis,
        spaced,
    )


def solution(mesh):
    shape = (mesh.shape["gx"], mesh.shape["gy"])
    in_specs = (
        P("gx", "gy"),
        P("gx", "gy"),
        P(),
        P("gx", "gy"),
        P("gx", "gy", None, None, None),
        P("gx", "gy", None, None, None),
        P(("gx", "gy"), None),
    )
    out_specs = (P("gx", "gy"), P("gx", "gy"), P("gx", "gy"))

    return jax.shard_map(
        functools.partial(per_device, shape),
        mesh=mesh,
        in_specs=in_specs,
        out_specs=out_specs,
        check_vma=False,
    )
```

time: 635 us -> 86 us (0.14)
  blocking collectives: 447 us -> 0 us
  starting transfers between devices: 123 us -> 0 us
  Pallas kernels: 0 us -> 76.1 us
  waiting for transfers between devices: 19.9 us -> 0 us
  other arithmetic: 11.6 us -> 0 us
  matrix products: 10.9 us -> 0 us
  between operations: 10.1 us -> 1.33 us
    unnamed x16 -> x0, blocking collectives: 224 us -> none
    psum x5 -> x0, blocking collectives: 223 us -> none  [the longest x3 134 us: precondition(): energy = lax.psum(jnp.sum(residual * result), ('gx', 'gy'))]
    ppermute x48 -> x0, starting transfers between devices: 123 us -> none  [the longest x24 92.6 us: extended_2(): before = lax.ppermute(last, axis, up)]
    pallas_call x0 -> x1, Pallas kernels: none -> 76.1 us  [per_device(): pl.pallas_call(functools.partial(kernel, shape), out_shape=(jax.ShapeDtyp...]
    ppermute x48 -> x0, waiting for transfers between devices: 19.9 us -> none  [the longest x24 19.8 us: extended_2(): before = lax.ppermute(last, axis, up)]
    dot_general x20 -> x0, matrix products: 10.9 us -> none  [the longest x4 4.07 us: precondition(): jnp.einsum('k,kxy->xy', weights, vectors, preferred_element_type=jnp.floa...]
  transfers between devices with their start and end apart: 48 -> 0, of which waited for: 18 -> 0; matrix products, arithmetic and copies ran while one was open for 0% -> 0% of each run, Pallas kernels for 0% -> 0%
where the time goes in v1:
time: 86 us; the launch traced here: 85.7 us
  Pallas kernels  76.1 us (88%)
  local copies, waits for them, and re-layouts  8.21 us (10%)
  between operations  1.33 us (2%)
    pallas_call x1, Pallas kernels, per_device(): pl.pallas_call(functools.partial(kernel, shape), out_shape=(jax.ShapeDtyp...  76.1 us
    unnamed x12, local copies, waits for them, and re-layouts  5.61 us

profile of v1, /device:TPU:0, one launch (start us, length us, event | category | flops | bytes accessed | tf_op | source)
XLA Modules:
  0.0 85.7 jit_solution(10051059815616375642)
XLA Ops:
  0.6 1.1 %reshape.20 = bf16[20,32,20]{2,1,0:T(8,128)(2,1)S(1)} reshape(bf16[20,640]{1,0:T(8,128)(2,1)} %param.13) | data formatting | bytes 51200 | tf_op jit(solution)/shard_map/reshape | solution.py:329
  1.8 0.1 copy.12
  1.9 1.4 %reshape.19 = bf16[20,4608]{1,0:T(8,128)(2,1)S(1)} reshape(bf16[1,1,20,32,144]{4,3,2,1,0:T(8,128)(2,1)} %param.12) | data formatting | bytes 368640 | tf_op jit(solution)/shard_map/reshape | solution.py:328
  4.0 0.0 copy-start
  4.0 1.7 %copy-done = bf16[1,1,18,256,256]{4,3,2,1,0:T(8,128)(2,1)S(1)} copy-done((bf16[1,1,18,256,256]{4,3,2,1,0:T(8,128)(2,1)S(1)}, bf16[1,1,18,256,256]{4,3,2,1,0:T(8,128)(2,1)}, u32[]{:S(2)}) %copy-start) | copy-done | bytes 2359320
  5.7 0.0 copy-start.1
  5.7 0.7 copy-done.1
  6.4 0.0 copy-start.2
  6.4 0.7 copy-done.2
  7.1 0.0 copy-start.3
  7.1 0.7 copy-done.3
  7.7 76.1 %shard_map.94 = (f32[16,128]{1,0:T(8,128)S(1)}, f32[16,128]{1,0:T(8,128)S(1)}, f32[16,128]{1,0:T(8,128)S(1)}) custom-call(f32[16,128]{1,0:T(8,128)S(1)} %copy-done.1, s32[16,128]{1,0:T(8,128)S(1)} %copy-done.2, f32[16]{0:T(128)S(1)} %copy-done.3, s32[1,1]{1,0:T(1,128)S(6)} %copy.16.kept_ref, bf16[18,256,256]{2,1,0:T(8,128)(2,1)S(1)} %bitcast.7, ...), custom_call_target="tpu_custom_call" | custom-call | tf_op jit(solution)/shard_map/pallas_call | solution.py:337
  83.9 0.6 copy.17
  84.5 0.6 copy.18
  85.1 0.6 copy.19
  (2 shorter events, 0.1 us)
Async XLA Ops:
  4.0 1.7 %copy-start = (bf16[1,1,18,256,256]{4,3,2,1,0:T(8,128)(2,1)S(1)}, bf16[1,1,18,256,256]{4,3,2,1,0:T(8,128)(2,1)}, u32[]{:S(2)}) copy-start(bf16[1,1,18,256,256]{4,3,2,1,0:T(8,128)(2,1)} %param.11) | copy-start | bytes 7077892
  5.7 0.7 copy-start.1
  6.4 0.7 copy-start.2
  7.1 0.7 copy-start.3

commit v2 on v1

--- a/solution.py
+++ b/solution.py
@@ -13,22 +13,31 @@
 MODES = 32
 MESH = pl.DeviceIdType.MESH
 SIDES = tuple((a, b) for a in (-1, 0, 1) for b in (-1, 0, 1) if (a, b) != (0, 0))
+TN = (((0,), (0,)), ((), ()))
 NT = (((1,), (1,)), ((), ()))
 NN = (((1,), (0,)), ((), ()))
 
 
 def kernel(
     shape,
+    right_in,
+    class_in,
+    values_ref,
+    kept_in,
+    factors_in,
+    basis_in,
+    coarse_in_ref,
+    out,
     right_ref,
     class_ref,
-    values_ref,
     kept_ref,
     factors_ref,
     basis_ref,
+    coarse_rows,
+    load_sems,
+    gram,
+    coarse_wide,
     coarse_ref,
-    field_out,
-    residual_out,
-    pre_out,
     cond,
     frames,
     fold,
@@ -52,14 +61,31 @@
     nx, ny = shape
     count = nx * ny
     rows, columns = right_ref.shape
+    modes = coarse_rows.shape[0]
     blocks, block = factors_ref.shape[:2]
     ext_rows, ext_columns = rows + 2 * OV, columns + 2 * OV
     ax, ay = lax.axis_index("gx"), lax.axis_index("gy")
     me = ax * ny + ay
     own = (pl.ds(rows, rows), pl.ds(columns, columns))
 
-    def place(number):
-        return (number // ny, number % ny)
+    loads = [
+        pltpu.make_async_copy(source, target, load_sems.at[index])
+        for index, (source, target) in enumerate(
+            (
+                (right_in, right_ref),
+                (class_in, class_ref),
+                (kept_in, kept_ref),
+                (coarse_in_ref, coarse_rows),
+                (factors_in, factors_ref),
+                (basis_in, basis_ref),
+            )
+        )
+    ]
+    for load in loads:
+        load.start()
+
+    def wrap(value, size):
+        return jnp.where(value >= size, value - size, value)
 
     def present(da, db):
         checks = []
@@ -85,9 +111,11 @@
 
     def fold_copy(slot, index):
         da, db = SIDES[index]
+        first, extent = (rows - OV if da < 0 else 0), (OV if da else rows)
+        lanes = pl.ds((1 + db) * columns, columns)
         return pltpu.make_async_remote_copy(
-            src_ref=patch(total, da, db),
-            dst_ref=fold.at[slot, index],
+            src_ref=total.at[slot, pl.ds((1 + da) * rows + first, extent), lanes],
+            dst_ref=fold.at[slot, index, pl.ds(first, extent)],
             send_sem=fold_send.at[slot, index],
             recv_sem=fold_recv.at[slot, index],
             device_id=(ax + da, ay + db),
@@ -115,23 +143,23 @@
             def _(index=index):
                 make(index).wait_send()
 
-    def gather_copy(slot, source, target):
+    def gather_copy(slot, tx, ty):
         return pltpu.make_async_remote_copy(
             src_ref=message.at[slot],
-            dst_ref=gathered.at[slot, source],
+            dst_ref=gathered.at[slot, me],
             send_sem=gather_send.at[slot],
             recv_sem=gather_recv.at[slot],
-            device_id=place(target),
+            device_id=(tx, ty),
             device_id_type=MESH,
         )
 
-    def scatter_copy(slot, source, target):
+    def scatter_copy(slot, tx, ty):
         return pltpu.make_async_remote_copy(
-            src_ref=terms.at[slot, target],
-            dst_ref=scattered.at[slot, source],
+            src_ref=terms.at[slot, tx * ny + ty],
+            dst_ref=scattered.at[slot, me],
             send_sem=scatter_send.at[slot],
             recv_sem=scatter_recv.at[slot],
-            device_id=place(target),
+            device_id=(tx, ty),
             device_id_type=MESH,
         )
 
@@ -142,22 +170,36 @@
             dst_ref=span,
             send_sem=send.at[slot],
             recv_sem=recv.at[slot],
-            device_id=place(lax.rem(me + 1, count)),
+            device_id=(wrap(ax + 1, nx), ay),
             device_id_type=MESH,
         )
 
     def others(act):
+        columns_of = [ay] + [wrap(ay + step, ny) for step in range(1, ny)]
+        for ty in columns_of[1:]:
+            act(ax, ty)
+
         def one(offset, carry):
-            act(lax.rem(me + offset, count))
+            tx = wrap(ax + offset, nx)
+            for ty in columns_of:
+                act(tx, ty)
             return carry
 
-        lax.fori_loop(1, count, one, 0)
+        lax.fori_loop(1, nx, one, 0)
 
     frames[...] = jnp.zeros_like(frames)
     cond[...] = jnp.zeros_like(cond)
     fold[...] = jnp.zeros_like(fold)
     total[...] = jnp.zeros_like(total)
+    barrier = pltpu.get_barrier_semaphore()
+    others(
+        lambda tx, ty: pl.semaphore_signal(
+            barrier, inc=1, device_id=(tx, ty), device_id_type=MESH
+        )
+    )
     natural[...] = jnp.zeros_like(natural)
+    for load in loads[:4]:
+        load.wait()
     right = right_ref[...]
     classes = class_ref[...]
     conductivity = jnp.zeros((rows, columns), jnp.float32)
@@ -165,17 +207,24 @@
         conductivity = jnp.where(classes == level, values_ref[level], conductivity)
     cond[own] = conductivity
     frames[(0,) + own] = right
-
-    barrier = pltpu.get_barrier_semaphore()
-    others(
-        lambda target: pl.semaphore_signal(
-            barrier, inc=1, device_id=place(target), device_id_type=MESH
-        )
-    )
+    coarse_wide[...] = jnp.zeros_like(coarse_wide)
+    narrow = coarse_rows[...].astype(jnp.float32)
+    for index in range(count):
+        coarse_wide[0:modes, index * LANES : index * LANES + modes] = narrow[
+            :, index * modes : (index + 1) * modes
+        ]
+    coarse_ref[...] = coarse_wide[...].astype(jnp.bfloat16)
     pl.semaphore_wait(barrier, count - 1)
 
     start_sides(lambda index: halo_copy(frames.at[0], 0, index))
     start_sides(lambda index: halo_copy(cond, ITERS + 1, index))
+    for load in loads[4:]:
+        load.wait()
+    for index in range(blocks):
+        factor = factors_ref[index]
+        gram[index] = lax.dot_general(
+            factor, factor, TN, preferred_element_type=jnp.float32
+        ).astype(jnp.bfloat16)
 
     frame_shape = cond.shape
     row_at = lax.broadcasted_iota(jnp.int32, frame_shape, 0) + (ax - 1) * rows
@@ -208,15 +257,12 @@
             row = jnp.where(lane == MODES + index, scalar, row)
         message[slot] = row
         message[slot, :, 0:MODES] = coarse_in * keep_modes
-        others(lambda target: gather_copy(slot, me, target).start())
+        others(lambda tx, ty: gather_copy(slot, tx, ty).start())
         gathered[slot, me] = message[slot]
         for index in range(blocks):
             at = slice(index * block, (index + 1) * block)
-            half = lax.dot_general(
-                box[:, at], factors_ref[index], NT, preferred_element_type=jnp.float32
-            ).astype(jnp.bfloat16)
             solved[0:1, at] = lax.dot_general(
-                half, factors_ref[index], NN, preferred_element_type=jnp.float32
+                box[:, at], gram[index], NN, preferred_element_type=jnp.float32
             )
         everything(gathered, gather_send, gather_recv, slot).wait_recv()
         sums = jnp.sum(gathered[slot], axis=0)
@@ -232,7 +278,7 @@
         )
         for index in range(count):
             terms[slot, index] = spread[:, index * LANES : (index + 1) * LANES]
-        others(lambda target: scatter_copy(slot, me, target).start())
+        others(lambda tx, ty: scatter_copy(slot, tx, ty).start())
         scattered[slot, me] = terms[slot, me]
         everything(scattered, scatter_send, scatter_recv, slot).wait_recv()
         coarse_out = jnp.sum(scattered[slot], axis=0) * keep
@@ -246,25 +292,22 @@
             ]
         lanes = lax.broadcasted_iota(jnp.int32, natural.shape, 1)
         clean = jnp.where(lanes < ext_columns, natural[...], 0.0)
-        total[rows - OV : rows - OV + ext_rows, :] = pltpu.roll(clean, columns - OV, 1)
+        total[slot, rows - OV : rows - OV + ext_rows, :] = pltpu.roll(clean, columns - OV, 1)
         copies = functools.partial(fold_copy, slot)
         start_sides(copies)
-        result = total[own]
+        result = total[(slot,) + own]
         wait_sides(copies)
         for index in range(len(SIDES)):
             result = result + fold[slot, index]
-        drain_sides(copies)
         return result, sums
 
     copies = lambda index: halo_copy(frames.at[0], 0, index)
     wait_sides(copies)
-    drain_sides(copies)
     zero = jnp.zeros((1, 1), jnp.float32)
     z, _ = precondition(0, frames[0], (zero,))
 
     copies = lambda index: halo_copy(cond, ITERS + 1, index)
     wait_sides(copies)
-    drain_sides(copies)
     cells = cond[...]
     face_north = 0.5 * (cells + pltpu.roll(cells, 1, 0))
     face_west = 0.5 * (cells + pltpu.roll(cells, 1, 1))
@@ -285,7 +328,6 @@
         copies = functools.partial(halo_copy, frames.at[step], step)
         start_sides(copies)
         wait_sides(copies)
-        drain_sides(copies)
         applied = operate(frames[step])
         applied_own = applied[rows : 2 * rows, columns : 2 * columns]
         scalars = [whole_sum(residual * z), whole_sum(z * applied_own)]
@@ -308,13 +350,16 @@
         residual = residual - length * image
         z = z - length * mapped
 
-    field_out[...] = field
-    residual_out[...] = residual
-    pre_out[...] = z
+    out[0] = field
+    out[1] = residual
+    out[2] = z
+    drain_sides(lambda index: halo_copy(cond, ITERS + 1, index))
 
     for slot in range(ITERS + 1):
         everything(gathered, gather_send, gather_recv, slot).wait_send()
         everything(terms, scatter_send, scatter_recv, slot).wait_send()
+        drain_sides(functools.partial(halo_copy, frames.at[slot], slot))
+        drain_sides(functools.partial(fold_copy, slot))
 
 
 def per_device(
@@ -326,24 +371,32 @@
     blocks, block = factors.shape[2:4]
     cells = blocks * block
     flat_basis = jnp.pad(basis.reshape(modes, cells), ((0, MODES - modes), (0, 0)))
-    spaced = coarse_factor.reshape(modes, count, modes)
-    spaced = jnp.pad(spaced, ((0, MODES - modes), (0, 0), (0, LANES - modes)))
-    spaced = spaced.reshape(MODES, count * LANES)
     steps = ITERS + 1
     frame = (3 * rows, 3 * columns)
     vmem = pl.BlockSpec(memory_space=pltpu.VMEM)
+    hbm = pl.BlockSpec(memory_space=pltpu.HBM)
     smem = pl.BlockSpec(memory_space=pltpu.SMEM)
-    f32 = jnp.float32
-    return pl.pallas_call(
+    f32, half = jnp.float32, jnp.bfloat16
+    stacked = pl.pallas_call(
         functools.partial(kernel, shape),
-        out_shape=(jax.ShapeDtypeStruct((rows, columns), f32),) * 3,
-        in_specs=[vmem, vmem, smem, vmem, vmem, vmem, vmem],
-        out_specs=(vmem,) * 3,
+        out_shape=jax.ShapeDtypeStruct((3, rows, columns), f32),
+        in_specs=[hbm, hbm, smem, hbm, hbm, hbm, hbm],
+        out_specs=vmem,
         scratch_shapes=[
+            pltpu.VMEM((rows, columns), f32),
+            pltpu.VMEM((rows, columns), jnp.int32),
+            pltpu.VMEM((1, 1), jnp.int32),
+            pltpu.VMEM((blocks, block, block), half),
+            pltpu.VMEM((MODES, cells), half),
+            pltpu.VMEM(coarse_factor.shape, half),
+            pltpu.SemaphoreType.DMA((6,)),
+            pltpu.VMEM((blocks, block, block), half),
+            pltpu.VMEM((MODES, count * LANES), f32),
+            pltpu.VMEM((MODES, count * LANES), half),
             pltpu.VMEM(frame, f32),
             pltpu.VMEM((steps,) + frame, f32),
             pltpu.VMEM((steps, len(SIDES), rows, columns), f32),
-            pltpu.VMEM(frame, f32),
+            pltpu.VMEM((steps,) + frame, f32),
             pltpu.VMEM((rows + 2 * OV, 3 * columns), f32),
             pltpu.VMEM((1, cells), f32),
             pltpu.VMEM((1, cells), f32),
@@ -370,8 +423,9 @@
         kept_counts,
         factors.reshape(blocks, block, block),
         flat_basis,
-        spaced,
+        coarse_factor,
     )
+    return (stacked[0], stacked[1], stacked[2])
 
 
 def solution(mesh):

time: 86 us -> 82.4 us (0.958)
  Pallas kernels: 76.1 us -> 74.2 us
  local copies, waits for them, and re-layouts: 8.21 us -> 6.52 us
    pallas_call x1, Pallas kernels: 76.1 us -> 74.2 us  [per_device(): pl.pallas_call(functools.partial(kernel, shape), out_shape=jax.ShapeDtype...]
    unnamed x12 -> x10, local copies, waits for them, and re-layouts: 5.61 us -> 4.46 us
    reshape x1 -> x0, local copies, waits for them, and re-layouts: 1.11 us -> none  [per_device(): spaced = coarse_factor.reshape(modes, count, modes)]
where the time goes in v2:
time: 82.4 us; the launch traced here: 82.1 us
  Pallas kernels  74.2 us (90%)
  local copies, waits for them, and re-layouts  6.52 us (8%)
  between operations  1.31 us (2%)
    pallas_call x1, Pallas kernels, per_device(): pl.pallas_call(functools.partial(kernel, shape), out_shape=jax.ShapeDtype...  74.2 us
    unnamed x10, local copies, waits for them, and re-layouts  4.46 us

profile of v2, /device:TPU:0, one launch (start us, length us, event | category | flops | bytes accessed | tf_op | source)
XLA Modules:
  0.0 82.1 jit_solution(17892833058200294350)
XLA Ops:
  0.6 1.4 %reshape.13 = bf16[20,4608]{1,0:T(8,128)(2,1)S(1)} reshape(bf16[1,1,20,32,144]{4,3,2,1,0:T(8,128)(2,1)} %param.12) | data formatting | bytes 368640 | tf_op jit(solution)/shard_map/reshape | solution.py:373
  2.7 0.0 copy-start
  2.8 1.7 %copy-done = bf16[1,1,18,256,256]{4,3,2,1,0:T(8,128)(2,1)S(1)} copy-done((bf16[1,1,18,256,256]{4,3,2,1,0:T(8,128)(2,1)S(1)}, bf16[1,1,18,256,256]{4,3,2,1,0:T(8,128)(2,1)}, u32[]{:S(2)}) %copy-start) | copy-done | bytes 2359320
  4.4 0.0 copy-start.1
  4.4 0.8 copy-done.1
  5.2 0.0 copy-start.2
  5.2 0.7 copy-done.2
  5.9 0.0 copy-start.3
  5.9 0.7 copy-done.3
  6.6 0.0 copy-start.4
  6.6 0.7 copy-done.4
  7.2 74.2 %shard_map.94 = f32[3,16,128]{2,1,0:T(8,128)S(1)} custom-call(f32[16,128]{1,0:T(8,128)S(1)} %copy-done.2, s32[16,128]{1,0:T(8,128)S(1)} %copy-done.3, f32[16]{0:T(128)S(1)} %copy-done.4, s32[1,1]{1,0:T(1,128)S(6)} %copy.10.kept_in, bf16[18,256,256]{2,1,0:T(8,128)(2,1)S(1)} %bitcast.9, bf16[32,4608]{1,0:T(8,128)(2,1)S(1)} %pad.4.basis_in, ...), custom_call_target="tpu_custom_call" | custom-call | tf_op jit(solution)/shard_map/pallas_call | solution.py:380
  81.5 0.6 slice_bitcast_fusion
  (1 shorter events, 0.0 us)
Async XLA Ops:
  2.7 1.7 %copy-start = (bf16[1,1,18,256,256]{4,3,2,1,0:T(8,128)(2,1)S(1)}, bf16[1,1,18,256,256]{4,3,2,1,0:T(8,128)(2,1)}, u32[]{:S(2)}) copy-start(bf16[1,1,18,256,256]{4,3,2,1,0:T(8,128)(2,1)} %param.11) | copy-start | bytes 7077892
  4.4 0.8 copy-start.1
  5.2 0.7 copy-start.2
  5.9 0.7 copy-start.3
  6.6 0.7 copy-start.4

commit v3 on v2

--- a/solution.py
+++ b/solution.py
@@ -176,16 +176,15 @@
 
     def others(act):
         columns_of = [ay] + [wrap(ay + step, ny) for step in range(1, ny)]
-        for ty in columns_of[1:]:
-            act(ax, ty)
-
         def one(offset, carry):
             tx = wrap(ax + offset, nx)
             for ty in columns_of:
                 act(tx, ty)
             return carry
 
-        lax.fori_loop(1, nx, one, 0)
+        lax.fori_loop(1, nx, one, 0, unroll=nx - 1 if nx <= 8 else 1)
+        for ty in columns_of[1:]:
+            act(ax, ty)
 
     frames[...] = jnp.zeros_like(frames)
     cond[...] = jnp.zeros_like(cond)
@@ -240,7 +239,7 @@
     def whole_sum(values):
         return jnp.sum(jnp.sum(values, axis=0, keepdims=True), axis=1, keepdims=True)
 
-    def precondition(slot, values, scalars):
+    def precondition(slot, values, pairs):
         wide = frame_shape[1]
         rolled = pltpu.roll(values, wide - (columns - OV), 1)
         natural[...] = rolled[rows - OV : rows - OV + ext_rows]
@@ -252,20 +251,19 @@
         coarse_in = lax.dot_general(
             box, basis_ref[...], NT, preferred_element_type=jnp.float32
         )
-        row = jnp.zeros((1, LANES), jnp.float32)
-        for index, scalar in enumerate(scalars):
-            row = jnp.where(lane == MODES + index, scalar, row)
-        message[slot] = row
+        message[slot] = jnp.zeros((1, LANES), jnp.float32)
         message[slot, :, 0:MODES] = coarse_in * keep_modes
         others(lambda tx, ty: gather_copy(slot, tx, ty).start())
         gathered[slot, me] = message[slot]
+        shares = jnp.zeros((1, LANES), jnp.float32)
+        for index, (first, second) in enumerate(pairs):
+            shares = jnp.where(lane == MODES + index, whole_sum(first * second), shares)
         for index in range(blocks):
             at = slice(index * block, (index + 1) * block)
             solved[0:1, at] = lax.dot_general(
                 box[:, at], gram[index], NN, preferred_element_type=jnp.float32
             )
         everything(gathered, gather_send, gather_recv, slot).wait_recv()
-        sums = jnp.sum(gathered[slot], axis=0)
         everyone = jnp.concatenate(
             [gathered[slot, index] for index in range(count)], axis=1
         ).astype(jnp.bfloat16)
@@ -277,11 +275,12 @@
             mid_half, coarse_ref[...], NN, preferred_element_type=jnp.float32
         )
         for index in range(count):
-            terms[slot, index] = spread[:, index * LANES : (index + 1) * LANES]
+            terms[slot, index] = spread[:, index * LANES : (index + 1) * LANES] + shares
         others(lambda tx, ty: scatter_copy(slot, tx, ty).start())
         scattered[slot, me] = terms[slot, me]
         everything(scattered, scatter_send, scatter_recv, slot).wait_recv()
-        coarse_out = jnp.sum(scattered[slot], axis=0) * keep
+        sums = jnp.sum(scattered[slot], axis=0)
+        coarse_out = sums * keep
         weights = coarse_out[:, :MODES].astype(jnp.bfloat16)
         solved[...] += lax.dot_general(
             weights, basis_ref[...], NN, preferred_element_type=jnp.float32
@@ -303,8 +302,7 @@
 
     copies = lambda index: halo_copy(frames.at[0], 0, index)
     wait_sides(copies)
-    zero = jnp.zeros((1, 1), jnp.float32)
-    z, _ = precondition(0, frames[0], (zero,))
+    z, _ = precondition(0, frames[0], ())
 
     copies = lambda index: halo_copy(cond, ITERS + 1, index)
     wait_sides(copies)
@@ -330,10 +328,10 @@
         wait_sides(copies)
         applied = operate(frames[step])
         applied_own = applied[rows : 2 * rows, columns : 2 * columns]
-        scalars = [whole_sum(residual * z), whole_sum(z * applied_own)]
+        pairs = [(residual, z), (z, applied_own)]
         if step > 1:
-            scalars.append(whole_sum(z * image))
-        corrected, sums = precondition(step, applied, scalars)
+            pairs.append((z, image))
+        corrected, sums = precondition(step, applied, pairs)
         fresh, plain = lane_value(sums, MODES), lane_value(sums, MODES + 1)
         if step == 1:
             direction, image, mapped, curvature = z, applied_own, corrected, plain
@@ -414,7 +412,7 @@
             pltpu.SemaphoreType.DMA((steps,)),
         ],
         compiler_params=pltpu.CompilerParams(
-            collective_id=0, has_side_effects=True, vmem_limit_bytes=40 * 2**20
+            collective_id=0, has_side_effects=True, vmem_limit_bytes=60 * 2**20
         ),
     )(
         right_side,

time: 82.4 us -> 79.6 us (0.966)
  local copies, waits for them, and re-layouts: 6.52 us -> 3.5 us
    unnamed x10 -> x0, local copies, waits for them, and re-layouts: 4.46 us -> none
where the time goes in v3:
time: 79.6 us; the launch traced here: 79.3 us
  Pallas kernels  74.5 us (94%)
  local copies, waits for them, and re-layouts  3.5 us (4%)
  between operations  1.29 us (2%)
    pallas_call x1, Pallas kernels, per_device(): pl.pallas_call(functools.partial(kernel, shape), out_shape=jax.ShapeDtype...  74.5 us

profile of v3, /device:TPU:0, one launch (start us, length us, event | category | flops | bytes accessed | tf_op | source)
XLA Modules:
  0.0 79.3 jit_solution(5991903395216519891)
XLA Ops:
  0.6 1.4 %reshape.13 = bf16[20,4608]{1,0:T(8,128)(2,1)S(1)} reshape(bf16[1,1,20,32,144]{4,3,2,1,0:T(8,128)(2,1)} %param.12) | data formatting | bytes 368640 | tf_op jit(solution)/shard_map/reshape | solution.py:371
  2.1 0.7 pad.4.basis_in
  3.4 74.5 %shard_map.94 = f32[3,16,128]{2,1,0:T(8,128)} custom-call(f32[16,128]{1,0:T(8,128)} %right_in.1, s32[16,128]{1,0:T(8,128)} %class_in.1, f32[16]{0:T(128)} %values_ref.1, s32[1,1]{1,0:T(1,128)S(6)} %copy.10.kept_in, bf16[18,256,256]{2,1,0:T(8,128)(2,1)} %bitcast.9, bf16[32,4608]{1,0:T(8,128)(2,1)} %pad.4.basis_in, bf16[20,640]{1,0:T(8,128)(2,1)} %coarse_in_ref.1), custom_call_target="tpu_custom_call" | custom-call | tf_op jit(solution)/shard_map/pallas_call | solution.py:378
  77.9 1.3 %slice_bitcast_fusion = (f32[16,128]{1,0:T(8,128)}, f32[16,128]{1,0:T(8,128)}, f32[16,128]{1,0:T(8,128)}) fusion(f32[3,16,128]{2,1,0:T(8,128)} %shard_map.94), kind=kLoop, calls=%fused_computation | loop fusion | bytes 49152 | tf_op jit(solution)/shard_map/squeeze | solution.py:426

commit v4 on v3

--- a/solution.py
+++ b/solution.py
@@ -136,13 +136,6 @@
             def _(index=index):
                 make(index).wait_recv()
 
-    def drain_sides(make):
-        for index, (da, db) in enumerate(SIDES):
-
-            @pl.when(present(da, db))
-            def _(index=index):
-                make(index).wait_send()
-
     def gather_copy(slot, tx, ty):
         return pltpu.make_async_remote_copy(
             src_ref=message.at[slot],
@@ -351,13 +344,18 @@
     out[0] = field
     out[1] = residual
     out[2] = z
-    drain_sides(lambda index: halo_copy(cond, ITERS + 1, index))
 
     for slot in range(ITERS + 1):
         everything(gathered, gather_send, gather_recv, slot).wait_send()
         everything(terms, scatter_send, scatter_recv, slot).wait_send()
-        drain_sides(functools.partial(halo_copy, frames.at[slot], slot))
-        drain_sides(functools.partial(fold_copy, slot))
+    for index, (da, db) in enumerate(SIDES):
+
+        @pl.when(present(da, db))
+        def _(index=index):
+            halo_copy(cond, ITERS + 1, index).wait_send()
+            for slot in range(ITERS + 1):
+                halo_copy(frames.at[slot], slot, index).wait_send()
+                fold_copy(slot, index).wait_send()
 
 
 def per_device(

time: 79.6 us -> 79.6 us (level)
  no operation moved by 1% of the time
where the time goes in v4:
time: 79.6 us; the launch traced here: 79.3 us
  Pallas kernels  74.5 us (94%)
  local copies, waits for them, and re-layouts  3.5 us (4%)
  between operations  1.29 us (2%)
    pallas_call x1, Pallas kernels, per_device(): pl.pallas_call(functools.partial(kernel, shape), out_shape=jax.ShapeDtype...  74.5 us

profile of v4, /device:TPU:0, one launch (start us, length us, event | category | flops | bytes accessed | tf_op | source)
XLA Modules:
  0.0 79.3 jit_solution(14619827265861235402)
XLA Ops:
  0.6 1.4 %reshape.13 = bf16[20,4608]{1,0:T(8,128)(2,1)S(1)} reshape(bf16[1,1,20,32,144]{4,3,2,1,0:T(8,128)(2,1)} %param.12) | data formatting | bytes 368640 | tf_op jit(solution)/shard_map/reshape | solution.py:369
  2.1 0.7 pad.4.basis_in
  3.4 74.5 %shard_map.94 = f32[3,16,128]{2,1,0:T(8,128)} custom-call(f32[16,128]{1,0:T(8,128)} %right_in.1, s32[16,128]{1,0:T(8,128)} %class_in.1, f32[16]{0:T(128)} %values_ref.1, s32[1,1]{1,0:T(1,128)S(6)} %copy.10.kept_in, bf16[18,256,256]{2,1,0:T(8,128)(2,1)} %bitcast.9, bf16[32,4608]{1,0:T(8,128)(2,1)} %pad.4.basis_in, bf16[20,640]{1,0:T(8,128)(2,1)} %coarse_in_ref.1), custom_call_target="tpu_custom_call" | custom-call | tf_op jit(solution)/shard_map/pallas_call | solution.py:376
  78.0 1.3 %slice_bitcast_fusion = (f32[16,128]{1,0:T(8,128)}, f32[16,128]{1,0:T(8,128)}, f32[16,128]{1,0:T(8,128)}) fusion(f32[3,16,128]{2,1,0:T(8,128)} %shard_map.94), kind=kLoop, calls=%fused_computation | loop fusion | bytes 49152 | tf_op jit(solution)/shard_map/squeeze | solution.py:424
